TPU v7x, 256 devices: a whole 4x4x8 slice. The times are simulated.
256 devices in a mesh: dp: 8 (over z), tensor: 8 (over y, core), seq: 4 (over x).
Axes of the slice: x: 4, y: 4, z: 8, core: 2. Of those that a mesh axis runs over, the one named last changes fastest.
Arguments:
- hidden: bfloat16 [5120, 16384], P('dp', 'tensor'), may hold values from -6 to 6
- query_weight: bfloat16 [16384, 8, 1024], P('tensor', None, 'seq'), may hold values from -0.046875 to 0.046875
- adapter_down_factor: bfloat16 [128, 64, 16384], P(('dp', 'seq'), None, 'tensor'), may hold values from -0.046875 to 0.046875
- adapter_up_factor: bfloat16 [128, 64, 8, 1024], P(('dp', 'seq'), None, 'tensor'), may hold values from -0.75 to 0.75
- adapter_pool_slot: int32 [128], replicated, may hold values from 0 to 127, as said below
- adapter_per_request: int32 [8, 32], P('dp'), may hold values from 0 to 127, as said below
- incoming_length: int32 [8, 32], P('dp'), may hold values from 1 to 64, 640 in all within a row
- prefix_page_table: int32 [8, 32, 16], P('dp'), may hold values from 0 to 63
- page_used_count: int32 [8, 32], P('dp'), may hold values from 1 to 16
- paged_key_cache: bfloat16 [8, 64, 64, 8, 128], P('dp', 'seq', None, 'tensor'), may hold values from -68 to 68
- paged_value_cache: bfloat16 [8, 64, 64, 8, 128], P('dp', 'seq', None, 'tensor'), may hold values from -6 to 6
- incoming_keys: bfloat16 [5120, 8, 128], P(('dp', 'seq'), 'tensor'), may hold values from -68 to 68
- incoming_values: bfloat16 [5120, 8, 128], P(('dp', 'seq'), 'tensor'), may hold values from -6 to 6
Outputs:
- attention: bfloat16 [5120, 8, 1024], P('dp', 'tensor', 'seq')
Inputs may be any that keep to these rules, and one draw needn't show every extreme that they name: Each slot appears once. The pool's slots are held in order by the devices of dp+seq, 4 slots each, so adapter a lies with holder adapter_pool_slot[a] // 4. `adapter_per_request`: among the 32 requests of one group, the named adapters lie with exactly 16 holders, each holding them for exactly 2 of the requests; one adapter may be named by several requests.
All inputs are finite; a program needn't handle non-finite values.
Results may differ from a plain program's by a relative error of at most 0.01.
The roundings to bfloat16 on the way count: a program that leaves them out, or rounds other values in their place, can miss the bound.
Values may be sent and summed in bfloat16 or wider, within the bound.
A program may use at most 128 MiB of HBM per device.

v0:
```python
import jax
import jax.numpy as jnp
from jax import lax
from jax.sharding import PartitionSpec as P

HEAD_WIDTH = 128
QUERY_GROUP = 8
CAP = 2
PAGE = 64


floor_score = -1e30


def membership(lengths, total_tokens):
    finish = jnp.cumsum(lengths)
    starts = finish - lengths
    position = jnp.arange(total_tokens, dtype=jnp.int32)
    member = (position[:, None] >= starts[None, :]) & (position[:, None] < finish[None, :])
    return (member, starts)


def page_membership(member, prefix_page_table, page_used_count, pool_pages):
    active = (
        jnp.arange(prefix_page_table.shape[1], dtype=jnp.int32)[None, :] < page_used_count[:, None]
    )
    listed = jnp.any(
        (prefix_page_table[:, :, None] == jnp.arange(pool_pages, dtype=jnp.int32)[None, None, :])
        & active[:, :, None],
        axis=1,
    )
    return jnp.any(member[:, :, None] & listed[None, :, :], axis=1)


def request_ids(member):
    return jnp.sum(
        jnp.where(member, jnp.arange(member.shape[1], dtype=jnp.int32)[None, :], 0), axis=1
    )


def owner_ranks(requests, adapter_pool_slot, count_per_holder):
    table_size = adapter_pool_slot.shape[0]
    slot_lookup = jnp.sum(
        jnp.where(
            requests[..., None] == jnp.arange(table_size, dtype=jnp.int32), adapter_pool_slot, 0
        ),
        axis=-1,
    )
    owners = slot_lookup // count_per_holder
    local_slot = slot_lookup - owners * count_per_holder
    positions = jnp.arange(requests.shape[-1], dtype=jnp.int32)
    earlier = (owners[..., :, None] == owners[..., None, :]) & (
        positions[None, :] < positions[:, None]
    )
    slot_rank = jnp.sum(earlier.astype(jnp.int32), axis=-1)
    return (owners, local_slot, slot_rank)


def attend(queries, key_rows, value_rows, allowed_keys):
    score_scale = queries.shape[-1] ** (-0.5)
    scores = (
        jnp.einsum("tlhd,kld->tlhk", queries, key_rows, preferred_element_type=jnp.float32)
        * score_scale
    )
    allowed = allowed_keys[:, None, None, :]
    masked = jnp.where(allowed, scores, floor_score)
    row_max = jnp.max(masked, axis=-1)
    weights = jnp.where(allowed, jnp.exp(masked - row_max[..., None]), 0.0)
    weight_sum = jnp.sum(weights, axis=-1)
    summed = jnp.einsum(
        "tlhk,kld->tlhd",
        weights.astype(jnp.bfloat16),
        value_rows,
        preferred_element_type=jnp.float32,
    )
    return (row_max, weight_sum, summed)


def body(
    hidden,
    query_weight,
    adapter_down_factor,
    adapter_up_factor,
    adapter_pool_slot,
    adapter_per_request,
    incoming_length,
    prefix_page_table,
    page_used_count,
    paged_key_cache,
    paged_value_cache,
    incoming_keys,
    incoming_values,
):
    groups = lax.axis_size("dp")
    sequence_count = lax.axis_size("seq")
    owner_count = groups * sequence_count
    seq_here = lax.axis_index("seq")
    owner_here = lax.axis_index("dp") * sequence_count + seq_here
    tokens_here, rows_all = hidden.shape
    requests = adapter_per_request.shape[1]
    count_per_holder, rank_extent = (adapter_down_factor.shape[0], adapter_down_factor.shape[1])
    local_key_value = adapter_up_factor.shape[2]
    head_columns = adapter_up_factor.shape[3]
    partial_columns = head_columns // sequence_count
    partial_rows = rows_all // sequence_count
    heads_part = QUERY_GROUP // sequence_count
    every_request = lax.all_gather(adapter_per_request, "dp", axis=0, tiled=True)
    owners, local_slot, slot_rank = owner_ranks(every_request, adapter_pool_slot, count_per_holder)
    capacity = jnp.arange(CAP, dtype=jnp.int32)
    adapter_pos = jnp.arange(count_per_holder, dtype=jnp.int32)
    picked = (
        (owners == owner_here)[:, None, :, None]
        & (slot_rank[:, None, :, None] == capacity[None, :, None, None])
        & (local_slot[:, None, :, None] == adapter_pos[None, None, None, :])
    )
    selector = jnp.any(picked, axis=2).astype(jnp.bfloat16)
    down_factor_blocks = adapter_down_factor.reshape(
        count_per_holder, rank_extent, sequence_count, partial_rows
    )
    down_send = jnp.einsum(
        "gck,krsx->gscrx", selector, down_factor_blocks, preferred_element_type=jnp.float32
    ).astype(jnp.bfloat16)
    up_factor_blocks = adapter_up_factor.reshape(
        count_per_holder, rank_extent, local_key_value, sequence_count, partial_columns
    )
    up_send = jnp.einsum(
        "gck,krlsp->gscrlp", selector, up_factor_blocks, preferred_element_type=jnp.float32
    ).astype(jnp.bfloat16)
    down_got, up_got = (
        lax.all_to_all(
            down_send.reshape(owner_count, CAP, rank_extent, partial_rows),
            ("dp", "seq"),
            split_axis=0,
            concat_axis=0,
            tiled=True,
        ),
        lax.all_to_all(
            up_send.reshape(owner_count, CAP, rank_extent, local_key_value, partial_columns),
            ("dp", "seq"),
            split_axis=0,
            concat_axis=0,
            tiled=True,
        ),
    )
    down_flat = down_got.reshape(owner_count * CAP, rank_extent, partial_rows)
    up_flat = up_got.reshape(owner_count * CAP, rank_extent, local_key_value * partial_columns)
    own_owner, own_slot, own_rank = owner_ranks(
        adapter_per_request[0], adapter_pool_slot, count_per_holder
    )
    chosen = own_owner * CAP + own_rank
    down_mine = jnp.take(down_flat, chosen, axis=0)
    up_mine = jnp.take(up_flat, chosen, axis=0)
    member, starts = membership(incoming_length[0], tokens_here)
    features = lax.dynamic_slice_in_dim(hidden, seq_here * partial_rows, partial_rows, 1)
    shrink_all = lax.dot_general(
        features,
        down_mine.reshape(requests * rank_extent, partial_rows),
        (((1,), (1,)), ((), ())),
        preferred_element_type=jnp.float32,
    )
    shrink_part = jnp.sum(
        shrink_all.reshape(tokens_here, requests, rank_extent)
        * member.astype(jnp.float32)[:, :, None],
        axis=1,
    )
    shrunk = lax.psum(shrink_part, ("tensor", "seq")).astype(jnp.bfloat16)
    spread_rows = (member.astype(jnp.bfloat16)[:, :, None] * shrunk[:, None, :]).reshape(
        tokens_here, requests * rank_extent
    )
    adapter_terms = jnp.dot(
        spread_rows,
        up_mine.reshape(requests * rank_extent, local_key_value * partial_columns),
        preferred_element_type=jnp.float32,
    )
    w_flat = query_weight.reshape(rows_all, -1)
    base_query = lax.psum_scatter(
        lax.dot_general(
            w_flat, hidden, (((0,), (1,)), ((), ())), preferred_element_type=jnp.float32
        ),
        "tensor",
        scatter_dimension=0,
        tiled=True,
    )
    queries = (
        (base_query.T + adapter_terms)
        .astype(jnp.bfloat16)
        .reshape(tokens_here, local_key_value, partial_columns)
    )
    local_pages = paged_key_cache.shape[1]
    page_mask = page_membership(
        member, prefix_page_table[0], page_used_count[0], local_pages * sequence_count
    )
    request_of = request_ids(member)
    positions = jnp.arange(tokens_here, dtype=jnp.int32)
    causal = (request_of[:, None] == request_of[None, :]) & (
        positions[None, :] <= positions[:, None]
    )
    pool_keys, pool_values, fresh_keys, fresh_values = (
        lax.all_gather(paged_key_cache, "seq", axis=1, tiled=True),
        lax.all_gather(paged_value_cache, "seq", axis=1, tiled=True),
        lax.all_gather(incoming_keys, "seq", axis=0, tiled=True),
        lax.all_gather(incoming_values, "seq", axis=0, tiled=True),
    )
    key_rows = jnp.concatenate(
        [pool_keys.reshape(-1, local_key_value, HEAD_WIDTH), fresh_keys], axis=0
    )
    value_rows = jnp.concatenate(
        [pool_values.reshape(-1, local_key_value, HEAD_WIDTH), fresh_values], axis=0
    )
    allowed_keys = jnp.concatenate([jnp.repeat(page_mask, PAGE, axis=1), causal], axis=1)
    row_max, weight_sum, summed = attend(
        queries.reshape(tokens_here, local_key_value, heads_part, HEAD_WIDTH),
        key_rows,
        value_rows,
        allowed_keys,
    )
    result = (
        (summed / weight_sum[..., None])
        .astype(jnp.bfloat16)
        .reshape(tokens_here, local_key_value, partial_columns)
    )
    return result


def solution(mesh):
    return jax.shard_map(
        body,
        mesh=mesh,
        in_specs=(
            P("dp", "tensor"),
            P("tensor", None, "seq"),
            P(("dp", "seq"), None, "tensor"),
            P(("dp", "seq"), None, "tensor", None),
            P(),
            P("dp", None),
            P("dp", None),
            P("dp", None, None),
            P("dp", None),
            P("dp", "seq", None, "tensor", None),
            P("dp", "seq", None, "tensor", None),
            P(("dp", "seq"), "tensor", None),
            P(("dp", "seq"), "tensor", None),
        ),
        out_specs=P("dp", "tensor", "seq"),
        check_vma=False,
    )
```

profile of v0, /device:TPU:1, one launch (start us, length us, event | category | flops | bytes accessed | tf_op | source)
XLA Modules:
  0.0 386.7 jit_solution(15373048443076217196)
XLA Ops:
  8.1 10.3 %copy.71 = bf16[256,8,8,256]{3,1,2,0:T(8,128)(2,1)} copy(bf16[256,8,8,256]{3,2,1,0:T(8,128)(2,1)} %bitcast.136) | data formatting | bytes 16777216
  18.5 10.8 %fusion.67 = f32[2048,640]{1,0:T(8,128)} fusion(bf16[2048,2048]{1,0:T(8,128)(2,1)} %bitcast.137, bf16[640,2048]{1,0:T(8,128)(2,1)S(1)} %copy-done), kind=kOutput, calls=%fused_computation.103 | convolution fusion | flops 5368709120 | bytes 16252928 | tf_op jit(solution)/shard_map/dot_general | solution.py:177
  29.9 16.1 %all-gather = s32[8,1,32]{2,1,0:T(1,128)S(1)} all-gather(s32[1,1,32]{2,1,0:T(1,128)S(1)} %bitcast.145), channel_id=1, replica_groups=mesh['dp'=8,'tensor'=8,'seq'=4] {'dp'}, dimensions={0}, use_global_device_ids=true | all-gather | bytes 1152 | tf_op jit(solution)/shard_map/all_gather | solution.py:107
  46.0 1.4 reshape.423
  49.4 2.5 copy.63
  51.9 6.7 %all-to-all-start.1 = ((bf16[32,2,64,1,256]{4,2,1,3,0:T(8,128)(2,1)}), bf16[32,2,64,1,256]{4,2,1,3,0:T(8,128)(2,1)}, u32[]{:S(2)}, u32[]{:S(2)}) async-start(bf16[32,2,64,1,256]{4,2,1,3,0:T(8,128)(2,1)} %bitcast.138), calls=%async_computation.2 | async-start | bytes 4194304 | tf_op jit(solution)/shard_map/all_to_all | solution.py:137
  58.6 2.7 reshape.420
  61.2 2.7 convert_bitcast_fusion
  63.9 4.4 %copy.61 = bf16[8,4,2,64,512]{4,3,2,1,0:T(8,128)(2,1)} copy(bf16[8,4,2,64,512]{4,0,1,3,2:T(8,128)(2,1)S(1)} %convert_bitcast_fusion) | data formatting | bytes 8388608 | tf_op jit(solution)/shard_map/convert_element_type | solution.py:122
  68.3 35.2 %all-to-all-done.1 = bf16[32,2,64,1,256]{4,2,1,3,0:T(8,128)(2,1)} async-done(((bf16[32,2,64,1,256]{4,2,1,3,0:T(8,128)(2,1)}), bf16[32,2,64,1,256]{4,2,1,3,0:T(8,128)(2,1)}, u32[]{:S(2)}, u32[]{:S(2)}) %all-to-all-start.1) | async-done | bytes 2097184 | tf_op jit(solution)/shard_map/all_to_all | solution.py:137
  103.5 8.1 %all-to-all-start = ((bf16[32,2,64,512]{3,2,1,0:T(8,128)(2,1)}), bf16[32,2,64,512]{3,2,1,0:T(8,128)(2,1)}, u32[]{:S(2)}, u32[]{:S(2)}) async-start(bf16[32,2,64,512]{3,2,1,0:T(8,128)(2,1)} %bitcast.134), calls=%async_computation.1 | async-start | bytes 8388608 | tf_op jit(solution)/shard_map/all_to_all | solution.py:130
  112.7 13.7 %all_gather.16 = bf16[640,1,128]{2,0,1:T(8,128)(2,1)S(1)} all-gather(bf16[160,1,128]{2,0,1:T(8,128)(2,1)S(1)} %copy-done.4), channel_id=1, replica_groups=mesh['dp'=8,'tensor'=8,'seq'=4] {'seq'}, dimensions={0}, use_global_device_ids=true | all-gather | bytes 204800 | tf_op jit(solution)/shard_map/all_gather | solution.py:202
  128.4 15.7 %all_gather.18 = bf16[640,1,128]{2,0,1:T(8,128)(2,1)S(1)} all-gather(bf16[160,1,128]{2,0,1:T(8,128)(2,1)S(1)} %copy-done.5), channel_id=1, replica_groups=mesh['dp'=8,'tensor'=8,'seq'=4] {'seq'}, dimensions={0}, use_global_device_ids=true | all-gather | bytes 204800 | tf_op jit(solution)/shard_map/all_gather | solution.py:201
  144.8 7.9 %pad_add_fusion = pred[640,4736]{0,1:T(8,128)(4,1)} fusion(pred[640,640]{0,1:T(8,128)(4,1)S(1)} %fusion.11, pred[640,4096]{0,1:T(8,128)(4,1)S(1)} %bitcast.135), kind=kLoop, calls=%fused_computation.9 | loop fusion | flops 3031040 | bytes 6062080 | tf_op jit(solution)/shard_map/concatenate | solution.py:210
  152.7 2.3 copy.55
  155.0 3.2 gather_fusion.1
  158.2 43.5 %all-to-all-done = bf16[32,2,64,512]{3,2,1,0:T(8,128)(2,1)} async-done(((bf16[32,2,64,512]{3,2,1,0:T(8,128)(2,1)}), bf16[32,2,64,512]{3,2,1,0:T(8,128)(2,1)}, u32[]{:S(2)}, u32[]{:S(2)}) %all-to-all-start) | async-done | bytes 4194336 | tf_op jit(solution)/shard_map/all_to_all | solution.py:130
  201.7 4.2 %gather_fusion = bf16[32,64,512]{2,1,0:T(8,128)(2,1)} fusion(bf16[64,64,512]{2,1,0:T(8,128)(2,1)} %bitcast.23, s32[1024]{0:T(1024)S(1)} %pad_clamp_fusion), kind=kCustom, calls=%fused_computation | custom fusion | bytes 4194432 | tf_op jit(solution)/shard_map/jit(_take)/gather | solution.py:151
  205.9 3.4 multiply_reduce_fusion
  209.4 128.8 %all-reduce.1 = bf16[640,64]{0,1:T(8,128)(2,1)S(1)} all-reduce(f32[640,64]{0,1:T(8,128)S(1)} %multiply_reduce_fusion), channel_id=1, replica_groups=mesh['dp'=8,'tensor'=8,'seq'=4] {'tensor','seq'}, use_global_device_ids=true, to_apply=%region_11.12 | all-reduce | flops 40960 | bytes 245760 | tf_op jit(solution)/shard_map/psum | solution.py:166
  338.2 2.5 fusion.23
  340.7 13.4 %fusion = (f32[640,2]{0,1:T(2,128)S(1)}, f32[4736,640,2]{1,0,2:T(8,128)}) fusion(pred[640,4736]{0,1:T(8,128)(4,1)} %pad_add_fusion, bf16[640,2,128]{0,2,1:T(8,128)(2,1)S(1)} %bitcast.150, bf16[640,1,128]{2,0,1:T(8,128)(2,1)S(1)} %all_gather.18, bf16[4096,1,128]{2,0,1:T(8,128)(2,1)} %bitcast.149), kind=kOutput, calls=%fused_computation.4 | convolution fusion | flops 1572502272 | bytes 28824576 | tf_op jit(solution)/shard_map/tlhd,kld->tlhk/dot_general | solution.py:62
  354.1 11.5 %fusion.1 = f32[640,2]{0,1:T(2,128)S(1)} fusion(f32[4736,640,2]{1,0,2:T(8,128)} %get-tuple-element.11, f32[640,2]{0,1:T(2,128)S(1)} %get-tuple-element.10, pred[640,4736]{0,1:T(8,128)(4,1)S(1)} %copy-done.2), kind=kLoop, calls=%fused_computation.5 | loop fusion | flops 30309120 | bytes 27289600 | tf_op jit(solution)/shard_map/reduce_sum | solution.py:69
  365.6 12.7 %fusion.39 = bf16[1,128,640,2]{2,1,3,0:T(8,128)(2,1)S(1)} fusion(f32[4736,640,2]{1,0,2:T(8,128)} %get-tuple-element.11, f32[640,2]{0,1:T(2,128)S(1)} %get-tuple-element.10, pred[640,4736]{0,1:T(8,128)(4,1)S(1)} %copy-done.2, bf16[640,1,128]{0,2,1:T(8,128)(2,1)S(1)} %copy.56, bf16[4096,1,128]{0,2,1:T(8,128)(2,1)S(1)} %copy-done.3, f32[640,2]{0,1:T(2,128)S(1)} %fusion.1), kind=kOutput, calls=%fused_computation.40 | convolution fusion | flops 1584955392 | bytes 28829696 | tf_op jit(solution)/shard_map/tlhk,kld->tlhd/dot_general | solution.py:70
  (60 shorter events, 7.9 us)
Async XLA Ops:
  7.4 11.1 %copy-start = (bf16[640,2048]{1,0:T(8,128)(2,1)S(1)}, bf16[640,2048]{1,0:T(8,128)(2,1)}, u32[]{:S(2)}) copy-start(bf16[640,2048]{1,0:T(8,128)(2,1)} %param.13) | copy-start | bytes 7864324
  7.4 145.3 %all-gather.4.cloned.1.call-start = ((), (), s32[]{:S(2)}) async-start(), calls=%async_computation.3 | async-start | bytes 1310720 | tf_op jit(solution)/shard_map/all_gather | solution.py:200
  8.1 330.1 %reduce-scatter.2.cloned.1.call-start = ((), (), s32[]{:S(2)}) async-start(), calls=%async_computation.5 | async-start | bytes 5898240 | tf_op jit(solution)/shard_map/reduce_scatter | solution.py:176
  29.2 0.7 copy-start.8
  29.2 18.2 %copy-start.7 = (s32[128]{0:T(128)S(1)}, s32[128]{0:T(128)}, u32[]{:S(2)}) copy-start(s32[128]{0:T(128)} %param.17) | copy-start | bytes 1540
  51.9 51.6 %all-to-all-start.1 = ((bf16[32,2,64,1,256]{4,2,1,3,0:T(8,128)(2,1)}), bf16[32,2,64,1,256]{4,2,1,3,0:T(8,128)(2,1)}, u32[]{:S(2)}, u32[]{:S(2)}) async-start(bf16[32,2,64,1,256]{4,2,1,3,0:T(8,128)(2,1)} %bitcast.138), calls=%async_computation.2 | async-start | bytes 4194304 | tf_op jit(solution)/shard_map/all_to_all | solution.py:137
  103.5 8.9 %copy-start.9 = (s32[1,32]{1,0:T(1,128)S(1)}, s32[1,32]{1,0:T(1,128)}, u32[]{:S(2)}) copy-start(s32[1,32]{1,0:T(1,128)} %param.19) | copy-start | bytes 388
  103.5 9.1 %copy-start.6 = (s32[1,32,16]{1,2,0:T(8,128)S(1)}, s32[1,32,16]{1,2,0:T(8,128)}, u32[]{:S(2)}) copy-start(s32[1,32,16]{1,2,0:T(8,128)} %param.20) | copy-start | bytes 6148
  103.5 9.2 %copy-start.4 = (bf16[160,1,128]{2,0,1:T(8,128)(2,1)S(1)}, bf16[160,1,128]{2,0,1:T(8,128)(2,1)}, u32[]{:S(2)}) copy-start(bf16[160,1,128]{2,0,1:T(8,128)(2,1)} %param.25) | copy-start | bytes 122884
  103.5 23.6 %copy-start.10 = (s32[1,32]{1,0:T(1,128)S(1)}, s32[1,32]{1,0:T(1,128)}, u32[]{:S(2)}) copy-start(s32[1,32]{1,0:T(1,128)} %param.21) | copy-start | bytes 388
  103.5 24.9 %copy-start.5 = (bf16[160,1,128]{2,0,1:T(8,128)(2,1)S(1)}, bf16[160,1,128]{2,0,1:T(8,128)(2,1)}, u32[]{:S(2)}) copy-start(bf16[160,1,128]{2,0,1:T(8,128)(2,1)} %param.24) | copy-start | bytes 122884
  103.5 98.2 %all-to-all-start = ((bf16[32,2,64,512]{3,2,1,0:T(8,128)(2,1)}), bf16[32,2,64,512]{3,2,1,0:T(8,128)(2,1)}, u32[]{:S(2)}, u32[]{:S(2)}) async-start(bf16[32,2,64,512]{3,2,1,0:T(8,128)(2,1)} %bitcast.134), calls=%async_computation.1 | async-start | bytes 8388608 | tf_op jit(solution)/shard_map/all_to_all | solution.py:130
  111.6 229.1 %all-gather.6.cloned.1.call-start = ((), (), s32[]{:S(2)}) async-start(), calls=%async_computation.4 | async-start | bytes 1310720 | tf_op jit(solution)/shard_map/all_gather | solution.py:199
  340.7 13.4 %copy-start.2 = (pred[640,4736]{0,1:T(8,128)(4,1)S(1)}, pred[640,4736]{0,1:T(8,128)(4,1)}, u32[]{:S(2)}) copy-start(pred[640,4736]{0,1:T(8,128)(4,1)} %pad_add_fusion) | copy-start | bytes 9093124
  354.1 11.5 %copy-start.3 = (bf16[4096,1,128]{0,2,1:T(8,128)(2,1)S(1)}, bf16[4096,1,128]{0,2,1:T(8,128)(2,1)}, u32[]{:S(2)}) copy-start(bf16[4096,1,128]{0,2,1:T(8,128)(2,1)} %copy.55) | copy-start | bytes 3145732
  365.6 13.7 %copy-start.1 = (bf16[640,2048]{1,0:T(8,128)(2,1)S(1)}, bf16[640,2048]{1,0:T(8,128)(2,1)}, u32[]{:S(2)}) copy-start(bf16[640,2048]{1,0:T(8,128)(2,1)} %param.13) | copy-start | bytes 7864324
Sparse Core Ops, SparseCore 0:
  10.0 29.3 all-gather.3
  114.3 41.9 all-gather.5
Sparse Core Ops, SparseCore 1:
  29.3 43.6 reduce-scatter.1
where the time goes:
time: 389 us; the launch traced here: 387 us
  blocking collectives  174 us (45%)
  waiting for transfers between devices  80.2 us (21%)
  matrix products  46.5 us (12%)
  local copies, waits for them, and re-layouts  33.6 us (9%)
  other arithmetic  22.2 us (6%)
  between operations  15.1 us (4%)
  starting transfers between devices  14.8 us (4%)
    psum x1, blocking collectives, body(): shrunk = lax.psum(shrink_part, ('tensor', 'seq')).astype(jnp.bfloat16)  129 us
    all_to_all x1, waiting for transfers between devices, body(): lax.all_to_all(down_send.reshape(owner_count, CAP, rank_extent, partial_r...  43.5 us
    all_to_all x1, waiting for transfers between devices, body(): lax.all_to_all(up_send.reshape(owner_count, CAP, rank_extent, local_key_v...  35.2 us
    all_gather x1, blocking collectives, body(): lax.all_gather(adapter_per_request, 'dp', axis=0, tiled=True)  16.1 us
    all_gather x1, blocking collectives, body(): lax.all_gather(incoming_keys, 'seq', axis=0, tiled=True)  15.7 us
    all_gather x1, blocking collectives, body(): lax.all_gather(incoming_values, 'seq', axis=0, tiled=True)  13.7 us
    dot_general x1, matrix products, attend(): jnp.einsum('tlhd,kld->tlhk', queries, key_rows, preferred_element_type=jn...  13.4 us
    dot_general x1, matrix products, attend(): jnp.einsum('tlhk,kld->tlhd', weights.astype(jnp.bfloat16), value_rows, pr...  12.7 us
  transfers between devices with their start and end apart: 5, of which 2 were waited for; matrix products, arithmetic and copies ran while one was open for 16% of the time, Pallas kernels for 0%

commit v1 on v0

v1 whole, which is shorter than its diff:
```python
import functools
import math

import jax
import jax.numpy as jnp
from jax import lax
from jax.experimental import pallas as pl
from jax.experimental.pallas import tpu as pltpu
from jax.sharding import PartitionSpec as P

MESH = pl.DeviceIdType.MESH
BF16, F32, I32 = jnp.bfloat16, jnp.float32, jnp.int32

TOK = 640
HALF = 320
WIDTH = 2048
QUARTER = 512
COLS = 256
HEAD = 128
RANK = 64
KEYS = 4096
NEW_EACH = 160
WINDOW = 192
CHUNK = 512
TILE = 320
NEGATIVE = -1e30
EXPONENT = HEAD**-0.5 * math.log2(math.e)


def lanes(rows):
    return lax.broadcasted_iota(I32, (rows, 128), 1)


def token_slots(meta, first, rows):
    position = lax.broadcasted_iota(I32, (rows, 128), 0) + first
    inside = (position >= meta[0:1, :]) & (position < meta[1:2, :])
    slot = jnp.where(inside, meta[2:3, :].astype(F32), 0.0)
    return jnp.broadcast_to(jnp.sum(slot, axis=1, keepdims=True), (rows, 128)).astype(I32)


def kernel(
    hidden,
    weight,
    down,
    up,
    meta,
    pages,
    cache_k,
    cache_v,
    new_k,
    new_v,
    out,
    hid,
    chunks,
    wraw,
    wf32,
    wk,
    downs,
    ups,
    metas,
    part_send,
    part_core,
    part_sum,
    part_y,
    query,
    shr,
    shr_core,
    shr_sum,
    shr_y,
    shr_own,
    shr_x,
    shr_all,
    shr_z,
    shr_final,
    shr_packed,
    shr_wide,
    slots_here,
    bias,
    keys,
    values,
    scores,
    load_sem,
    w_sem,
    meta_s,
    meta_r,
    hid_s,
    hid_r,
    up_s,
    up_r,
    x_s,
    x_r,
    core_s,
    core_r,
    y_s,
    y_r,
    red_s,
    red_r,
):
    z = lax.axis_index("dp")
    t = lax.axis_index("tensor")
    x = lax.axis_index("seq")
    y, core = t // 2, t % 2

    def at_z(d):
        return {"dp": lax.rem(z + d + 8, 8)}

    def at_x(d):
        return {"seq": lax.rem(x + d, 4)}

    def at_y(d):
        return {"tensor": lax.rem(y + d, 4) * 2 + core}

    sibling = {"tensor": y * 2 + 1 - core}
    barrier = pltpu.get_barrier_semaphore()
    peers = [at_z(d) for d in range(1, 8)] + [at_x(d) for d in range(1, 4)]
    peers += [at_y(d) for d in range(1, 4)] + [sibling]
    for peer in peers:
        pl.semaphore_signal(barrier, inc=1, device_id=peer, device_id_type=MESH)
    pl.semaphore_wait(barrier, len(peers))

    def send(src, dst, s, r, peer):
        copy = pltpu.make_async_remote_copy(
            src_ref=src, dst_ref=dst, send_sem=s, recv_sem=r, device_id=peer, device_id_type=MESH
        )
        copy.start()
        return copy

    def local(src, dst, sem):
        copy = pltpu.make_async_copy(src, dst, sem)
        copy.start()
        return copy

    pending = []
    quarter = pl.ds(pl.multiple_of(x * QUARTER, QUARTER), QUARTER)

    ring = {}
    for u in range(2):
        rows = pl.ds(u * HALF, HALF)
        for way in range(2):
            ring[way, 1, u] = send(
                hidden.at[rows, quarter],
                chunks.at[z, rows],
                hid_s.at[way, 0, u],
                hid_r.at[way, 0, u],
                at_z(1 - 2 * way),
            )
    meta_copies = [
        send(meta, metas.at[z], meta_s.at[d], meta_r.at[d], at_z(d)) for d in range(1, 8)
    ]
    own = [local(meta, metas.at[z], load_sem.at[0])]
    own_hid = local(hidden, hid, load_sem.at[1])
    own_chunk = local(hidden.at[:, quarter], chunks.at[z], load_sem.at[2])
    w_copies = [
        local(weight.at[pl.ds(i * 256, 256)], wraw.at[pl.ds(i * 256, 256)], w_sem.at[i])
        for i in range(8)
    ]
    mine4 = pl.ds(x * 4, 4)
    down_copies = []
    for d in range(1, 4):
        to = lax.rem(x + d, 4)
        down_copies.append(
            send(
                down.at[:, :, pl.ds(pl.multiple_of(to * QUARTER, QUARTER), QUARTER)],
                downs.at[mine4],
                x_s.at[0, d],
                x_r.at[0, d],
                at_x(d),
            )
        )
    own_down = local(down.at[:, :, quarter], downs.at[mine4], load_sem.at[3])
    up_copies = []
    for h in range(2):
        for d in range(1, 4):
            to = lax.rem(x + d, 4)
            up_copies.append(
                send(
                    up.at[:, :, pl.ds(pl.multiple_of(to * COLS + h * HEAD, HEAD), HEAD)],
                    ups.at[z, h, mine4],
                    x_s.at[1 + h, d],
                    x_r.at[1 + h, d],
                    at_x(d),
                )
            )
        own.append(
            local(
                up.at[:, :, pl.ds(pl.multiple_of(x * COLS + h * HEAD, HEAD), HEAD)],
                ups.at[z, h, mine4],
                load_sem.at[4 + h],
            )
        )

    def serve_hidden(step, u):
        rows = pl.ds(u * HALF, HALF)
        for way in range(2):
            if step == 4 and u != way:
                continue
            ring[way, step, u].wait_recv()
            if step < 3 or (step == 3 and u == way):
                origin = lax.rem(z + (2 * way - 1) * step + 8, 8)
                ring[way, step + 1, u] = send(
                    chunks.at[origin, rows],
                    chunks.at[origin, rows],
                    hid_s.at[way, step, u],
                    hid_r.at[way, step, u],
                    at_z(1 - 2 * way),
                )

    up_ring = {}

    def up_part(origin, h, r):
        return ups.at[origin, h, pl.ds(r * 8, 8)]

    def start_up(h, r):
        for way in range(2):
            up_ring[way, 1, h, r] = send(
                up_part(z, h, r),
                up_part(z, h, r),
                up_s.at[way, 0, h, r],
                up_r.at[way, 0, h, r],
                at_z(1 - 2 * way),
            )

    def serve_up(step, h, r):
        for way in range(2):
            if step == 4 and r != way:
                continue
            up_ring[way, step, h, r].wait_recv()
            if step < 3 or (step == 3 and r == way):
                origin = lax.rem(z + (2 * way - 1) * step + 8, 8)
                up_ring[way, step + 1, h, r] = send(
                    up_part(origin, h, r),
                    up_part(origin, h, r),
                    up_s.at[way, step, h, r],
                    up_r.at[way, step, h, r],
                    at_z(1 - 2 * way),
                )

    for i in range(8):
        w_copies[i].wait()

    @pl.loop(0, 16)
    def _(i):
        first = pl.multiple_of(i * 128, 128)
        wide = wraw[pl.ds(first, 128)].astype(F32).reshape(1024, COLS)
        wf32[pl.ds(0, 1024)] = wide[:, :HEAD]
        wf32[pl.ds(1024, 1024)] = wide[:, HEAD:]
        for k in range(8):
            for g in range(2):
                wk[k, pl.ds(first, 128), pl.ds(g * HEAD, HEAD)] = wf32[
                    pl.ds(g * 1024 + k, 128, stride=8), :
                ].astype(BF16)

    own_hid.wait()

    def product(head, rows):
        return jnp.dot(hid[rows], wk[head], preferred_element_type=F32)

    part_copies = []
    for d in range(4):
        target = lax.rem(y + 1 + d, 4)

        @pl.loop(0, 2)
        def _(i):
            rows = pl.ds(pl.multiple_of(i * HALF, HALF), HALF)
            part_send[d, rows] = product(target * 2 + 1 - core, rows)

        part_copies.append(
            send(part_send.at[d], part_core.at[d], core_s.at[d], core_r.at[d], sibling)
        )
    serve_hidden(1, 0)
    y_copies = []
    for d in range(4):
        target = lax.rem(y + 1 + d, 4)
        part_copies[d].wait_recv()

        @pl.loop(0, 2)
        def _(i):
            rows = pl.ds(pl.multiple_of(i * HALF, HALF), HALF)
            part_sum[d, rows] = product(target * 2 + core, rows) + part_core[d, rows]

        if d < 3:
            y_copies.append(
                send(part_sum.at[d], part_y.at[d], y_s.at[d], y_r.at[d], at_y(1 + d))
            )
    serve_hidden(1, 1)

    for copy in meta_copies:
        copy.wait_recv()
    own[0].wait()
    own_down.wait()
    own_chunk.wait()
    for copy in down_copies:
        copy.wait_recv()

    def shrink(origin):
        origin = lax.rem(origin + 8, 8)
        about = metas[origin]

        def block(first):
            rows = pl.ds(first, 160)
            product = lax.dot_general(
                chunks[origin, rows],
                downs[...].reshape(1024, QUARTER),
                (((1,), (1,)), ((), ())),
                preferred_element_type=F32,
            )
            slot = token_slots(about, first, 160) - z * 16
            half = lanes(160) // RANK
            total = jnp.zeros((160, 128), F32)
            for j in range(8):
                piece = product[:, j * 128 : (j + 1) * 128]
                total = total + jnp.where(slot == 2 * j + half, piece, 0.0)
            return total + pltpu.roll(total, RANK, 1)

        @pl.loop(0, 2)
        def _(i):
            first = pl.multiple_of(i * 160, 160)
            low, high = block(first), block(first + HALF)
            shr[origin, pl.ds(first, 160)] = jnp.where(lanes(160) < RANK, low, high)

    shrink(z)
    shrink(z - 1)
    serve_hidden(2, 0)
    shrink(z + 1)
    own[1].wait()
    own[2].wait()
    for copy in up_copies:
        copy.wait_recv()

    kv_copies = []
    mine_old = pl.ds(pl.multiple_of(x * 1024, 1024), 1024)
    mine_new = pl.ds(pl.multiple_of(KEYS + x * NEW_EACH, 32), NEW_EACH)
    first_lanes = pl.ds(0, HEAD)
    for n, (src, dst) in enumerate(
        (
            (cache_k, keys.at[mine_old, first_lanes]),
            (cache_v, values.at[mine_old]),
            (new_k, keys.at[mine_new, first_lanes]),
            (new_v, values.at[mine_new]),
        )
    ):
        for d in range(1, 4):
            kv_copies.append(send(src, dst, x_s.at[3 + n, d], x_r.at[3 + n, d], at_x(d)))
        own.append(local(src, dst, load_sem.at[6 + n]))
    serve_hidden(2, 1)
    shrink(z - 2)
    shrink(z + 2)

    about = metas[z]
    place = lanes(32)
    listed = jnp.zeros((32, 128), F32)
    for i in range(16):
        listed = jnp.maximum(listed, jnp.where(pages[:, i : i + 1] == place, 1.0, 0.0))
    same = place - 64 == lax.broadcasted_iota(I32, (32, 128), 0)
    listed = jnp.where(same, 1.0, listed)
    listed = jnp.concatenate([listed, jnp.zeros((96, 128), F32)], axis=0).astype(BF16)

    @pl.loop(0, 4)
    def _(i):
        first = pl.multiple_of(i * 160, 160)
        rows = pl.ds(first, 160)
        position = lax.broadcasted_iota(I32, (160, 128), 0) + first
        member = (position >= about[0:1, :]) & (position < about[1:2, :])
        count = jnp.dot(
            jnp.where(member, 1.0, 0.0).astype(BF16), listed, preferred_element_type=F32
        )
        free = (count > 0.5) | (lanes(160) >= 96)
        bias[rows] = jnp.where(free, 0.0, NEGATIVE).astype(BF16)
        slots_here[rows] = token_slots(about, first, 160)
        shifted = (position >= about[3:4, :]) & (position < about[4:5, :])
        keys[pl.ds(pl.multiple_of(KEYS + i * 160, 32), 160), pl.ds(HEAD, 128)] = jnp.where(
            shifted, 1.0, 0.0
        ).astype(BF16)

    @pl.loop(0, 16)
    def _(i):
        first = pl.multiple_of(i * 256, 256)
        page = (lax.broadcasted_iota(I32, (256, 128), 0) + first) // 64
        keys[pl.ds(first, 256), pl.ds(HEAD, 128)] = jnp.where(
            page == lanes(256), 1.0, 0.0
        ).astype(BF16)

    serve_hidden(3, 0)
    start_up(0, 0)
    start_up(0, 1)
    for copy in y_copies:
        copy.wait_recv()

    @pl.loop(0, 2)
    def _(i):
        rows = pl.ds(pl.multiple_of(i * HALF, HALF), HALF)
        total = part_sum[3, rows] + part_y[0, rows] + part_y[1, rows] + part_y[2, rows]
        query[0, rows] = total[:, :HEAD]
        query[1, rows] = total[:, HEAD:]

    serve_hidden(3, 1)
    shrink(z - 3)
    shrink(z + 3)
    serve_hidden(4, 0)
    serve_hidden(4, 1)
    shrink(z + 4)

    other_rows = pl.ds(pl.multiple_of((1 - core) * 160, 32), 160)
    core_rows = pl.ds(pl.multiple_of(core * 160, 32), 160)
    core_copy = send(shr.at[:, other_rows], shr_core, red_s.at[0, 0], red_r.at[0, 0], sibling)
    serve_up(1, 0, 0)
    core_copy.wait_recv()
    shr_sum[...] = shr[:, core_rows] + shr_core[...]
    red_y = []
    for d in range(1, 4):
        rows = pl.ds(pl.multiple_of(lax.rem(y + d, 4) * 40, 8), 40)
        red_y.append(
            send(shr_sum.at[:, rows], shr_y.at[d - 1], red_s.at[1, d], red_r.at[1, d], at_y(d))
        )
    serve_up(1, 0, 1)
    serve_up(2, 0, 0)
    for copy in red_y:
        copy.wait_recv()
    shr_own[...] = (
        shr_sum[:, pl.ds(pl.multiple_of(y * 40, 8), 40)] + shr_y[0] + shr_y[1] + shr_y[2]
    )
    red_x = [
        send(shr_own, shr_x.at[x], red_s.at[2, d], red_r.at[2, d], at_x(d)) for d in range(1, 4)
    ]
    shr_x[x] = shr_own[...]
    start_up(1, 0)
    start_up(1, 1)
    serve_up(2, 0, 1)
    serve_up(3, 0, 0)
    for copy in red_x:
        copy.wait_recv()
    shr_all[...] = (shr_x[0] + shr_x[1] + shr_x[2] + shr_x[3]).astype(BF16).astype(F32)
    red_z = [
        send(
            shr_all.at[lax.rem(z + d, 8)], shr_z.at[d - 1], red_s.at[3, d], red_r.at[3, d], at_z(d)
        )
        for d in range(1, 8)
    ]
    serve_up(3, 0, 1)
    for copy in red_z:
        copy.wait_recv()
    total = shr_all[z]
    for d in range(7):
        total = total + shr_z[d]
    shr_final[...] = total
    final_rows = pl.ds(pl.multiple_of(core * 160 + y * 40, 8), 40)
    red_f = [
        send(
            shr_final, shr_packed.at[final_rows], red_s.at[4, d], red_r.at[4, d], at_y(d)
        )
        for d in range(1, 4)
    ]
    shr_packed[final_rows] = total
    for copy in red_f:
        copy.wait_recv()
    core_final = send(
        shr_packed.at[core_rows], shr_packed.at[core_rows], red_s.at[0, 1], red_r.at[0, 1], sibling
    )
    serve_up(4, 0, 0)
    serve_up(4, 0, 1)
    core_final.wait_recv()
    packed = shr_packed[...]
    turned = pltpu.roll(packed, RANK, 1)
    shr_wide[pl.ds(0, HALF)] = jnp.where(lanes(HALF) < RANK, packed, turned)
    shr_wide[pl.ds(HALF, HALF)] = jnp.where(lanes(HALF) < RANK, turned, packed)

    def expand(origin, h):
        origin = lax.rem(origin + 8, 8)

        @pl.loop(0, 4)
        def _(i):
            rows = pl.ds(pl.multiple_of(i * 160, 160), 160)
            slot = slots_here[rows] - origin * 16
            wide = shr_wide[rows]
            half = lanes(160) // RANK
            spread = jnp.concatenate(
                [jnp.where(slot == 2 * j + half, wide, 0.0).astype(BF16) for j in range(8)], axis=1
            )
            query[h, rows] += jnp.dot(
                spread, ups[origin, h].reshape(1024, HEAD), preferred_element_type=F32
            )

    def attend(h):
        @pl.loop(0, TOK // TILE)
        def _(i):
            first = pl.multiple_of(i * TILE, TILE)
            rows = pl.ds(first, TILE)
            left = jnp.concatenate([query[h, rows].astype(BF16), bias[rows]], axis=1)
            highest = jnp.full((TILE, 128), NEGATIVE, F32)
            for c in range(KEYS // CHUNK):
                piece = lax.dot_general(
                    left,
                    keys[pl.ds(c * CHUNK, CHUNK)],
                    (((1,), (1,)), ((), ())),
                    preferred_element_type=F32,
                )
                scores[:, pl.ds(c * CHUNK, CHUNK)] = piece
                for j in range(CHUNK // 128):
                    highest = jnp.maximum(highest, piece[:, j * 128 : (j + 1) * 128])
            piece = lax.dot_general(
                left,
                keys[pl.ds(KEYS, TOK)],
                (((1,), (1,)), ((), ())),
                preferred_element_type=F32,
            )
            position = lax.broadcasted_iota(I32, (TILE, TOK), 0) + first
            piece = jnp.where(
                lax.broadcasted_iota(I32, (TILE, TOK), 1) <= position, piece, NEGATIVE
            )
            scores[:, pl.ds(KEYS, TOK)] = piece
            for j in range(TOK // 128):
                highest = jnp.maximum(highest, piece[:, j * 128 : (j + 1) * 128])
            top = jnp.broadcast_to(jnp.max(highest, axis=1, keepdims=True), (TILE, 128))
            sums = jnp.zeros((TILE, 128), F32)
            total = jnp.zeros((TILE, HEAD), F32)
            bounds = [(c * CHUNK, CHUNK) for c in range(KEYS // CHUNK)] + [(KEYS, TOK)]
            for begin, size in bounds:
                parts = []
                for j in range(size // 128):
                    e = jnp.exp2((scores[:, pl.ds(begin + j * 128, 128)] - top) * EXPONENT)
                    sums = sums + e
                    parts.append(e.astype(BF16))
                total = total + jnp.dot(
                    jnp.concatenate(parts, axis=1),
                    values[pl.ds(begin, size)],
                    preferred_element_type=F32,
                )
            out[rows, pl.ds(h * HEAD, HEAD)] = (
                total / jnp.sum(sums, axis=1, keepdims=True)
            ).astype(BF16)

    for d in (0, -1, 1):
        expand(z + d, 0)
    serve_up(1, 1, 0)
    serve_up(1, 1, 1)
    for d in (-2, 2, -3, 3, 4):
        expand(z + d, 0)
    serve_up(2, 1, 0)
    serve_up(2, 1, 1)
    for copy in kv_copies:
        copy.wait_recv()
    for copy in own[3:]:
        copy.wait()
    for d in (0, -1, 1, -2, 2):
        expand(z + d, 1)
    serve_up(3, 1, 0)
    serve_up(3, 1, 1)
    for d in (-3, 3):
        expand(z + d, 1)
    attend(0)
    serve_up(4, 1, 0)
    serve_up(4, 1, 1)
    expand(z + 4, 1)
    attend(1)

    for copies in (
        list(ring.values()),
        list(up_ring.values()),
        meta_copies,
        down_copies,
        up_copies,
        part_copies,
        y_copies,
        kv_copies,
        [core_copy],
        red_y,
        red_x,
        red_z,
        red_f,
        [core_final],
    ):
        for copy in copies:
            copy.wait_send()


def body(
    hidden,
    query_weight,
    adapter_down_factor,
    adapter_up_factor,
    adapter_pool_slot,
    adapter_per_request,
    incoming_length,
    prefix_page_table,
    page_used_count,
    paged_key_cache,
    paged_value_cache,
    incoming_keys,
    incoming_values,
):
    lengths = incoming_length[0]
    finish = jnp.cumsum(lengths)
    starts = finish - lengths
    slots = jnp.sum(
        jnp.where(
            adapter_per_request[0][:, None] == jnp.arange(128, dtype=I32)[None, :],
            adapter_pool_slot[None, :],
            0,
        ),
        axis=1,
    )
    low = jnp.pad(jnp.stack([starts, finish, slots]), ((0, 5), (0, 96)))
    high = jnp.pad(jnp.stack([starts, finish]), ((3, 3), (64, 32)))
    meta = low + high
    pages = jnp.where(
        jnp.arange(16, dtype=I32)[None, :] < page_used_count[0][:, None], prefix_page_table[0], -1
    )
    vmem = pl.BlockSpec(memory_space=pltpu.VMEM)
    anywhere = pl.BlockSpec(memory_space=pl.ANY)
    dma = pltpu.SemaphoreType.DMA
    result = pl.pallas_call(
        kernel,
        out_shape=jax.ShapeDtypeStruct((TOK, COLS), BF16),
        in_specs=[anywhere] * 5 + [vmem] + [anywhere] * 4,
        out_specs=vmem,
        scratch_shapes=[
            pltpu.VMEM((TOK, WIDTH), BF16),
            pltpu.VMEM((8, TOK, QUARTER), BF16),
            pltpu.VMEM((WIDTH, 8, COLS), BF16),
            pltpu.VMEM((2048, HEAD), F32),
            pltpu.VMEM((8, WIDTH, COLS), BF16),
            pltpu.VMEM((16, RANK, QUARTER), BF16),
            pltpu.VMEM((8, 2, 16, RANK, HEAD), BF16),
            pltpu.VMEM((8, 8, 128), I32),
            pltpu.VMEM((4, TOK, COLS), F32),
            pltpu.VMEM((4, TOK, COLS), F32),
            pltpu.VMEM((4, TOK, COLS), F32),
            pltpu.VMEM((3, TOK, COLS), F32),
            pltpu.VMEM((2, TOK, HEAD), F32),
            pltpu.VMEM((8, HALF, 128), F32),
            pltpu.VMEM((8, 160, 128), F32),
            pltpu.VMEM((8, 160, 128), F32),
            pltpu.VMEM((3, 8, 40, 128), F32),
            pltpu.VMEM((8, 40, 128), F32),
            pltpu.VMEM((4, 8, 40, 128), F32),
            pltpu.VMEM((8, 40, 128), F32),
            pltpu.VMEM((7, 40, 128), F32),
            pltpu.VMEM((40, 128), F32),
            pltpu.VMEM((HALF, 128), F32),
            pltpu.VMEM((TOK, 128), F32),
            pltpu.VMEM((TOK, 128), I32),
            pltpu.VMEM((TOK, 128), BF16),
            pltpu.VMEM((KEYS + TOK, 2 * HEAD), BF16),
            pltpu.VMEM((KEYS + TOK, HEAD), BF16),
            pltpu.VMEM((TILE, KEYS + TOK), F32),
            dma((10,)),
            dma((8,)),
            dma((8,)),
            dma((8,)),
            dma((2, 4, 2)),
            dma((2, 4, 2)),
            dma((2, 4, 2, 2)),
            dma((2, 4, 2, 2)),
            dma((7, 4)),
            dma((7, 4)),
            dma((4,)),
            dma((4,)),
            dma((3,)),
            dma((3,)),
            dma((5, 8)),
            dma((5, 8)),
        ],
        compiler_params=pltpu.CompilerParams(
            collective_id=0, has_side_effects=True, vmem_limit_bytes=63 << 20
        ),
        name="layer",
    )(
        hidden,
        query_weight,
        adapter_down_factor,
        adapter_up_factor.reshape(4, RANK, 1024),
        meta,
        pages,
        paged_key_cache.reshape(1024, HEAD),
        paged_value_cache.reshape(1024, HEAD),
        incoming_keys.reshape(NEW_EACH, HEAD),
        incoming_values.reshape(NEW_EACH, HEAD),
    )
    return result.reshape(TOK, 1, COLS)


def solution(mesh):
    return jax.shard_map(
        body,
        mesh=mesh,
        in_specs=(
            P("dp", "tensor"),
            P("tensor", None, "seq"),
            P(("dp", "seq"), None, "tensor"),
            P(("dp", "seq"), None, "tensor", None),
            P(),
            P("dp", None),
            P("dp", None),
            P("dp", None, None),
            P("dp", None),
            P("dp", "seq", None, "tensor", None),
            P("dp", "seq", None, "tensor", None),
            P(("dp", "seq"), "tensor", None),
            P(("dp", "seq"), "tensor", None),
        ),
        out_specs=P("dp", "tensor", "seq"),
        check_vma=False,
    )
```

time: 389 us -> 148 us (0.38)
  blocking collectives: 174 us -> 0 us
  Pallas kernels: 0 us -> 141 us
  waiting for transfers between devices: 80.2 us -> 0 us
  matrix products: 46.5 us -> 0 us
  local copies, waits for them, and re-layouts: 33.6 us -> 2.49 us
  other arithmetic: 22.2 us -> 4.38 us
  between operations: 15.1 us -> 0.02 us
  starting transfers between devices: 14.8 us -> 0 us
    pallas_call x0 -> x1, Pallas kernels: none -> 141 us  [body(): pl.pallas_call(kernel, out_shape=jax.ShapeDtypeStruct((TOK, COLS), BF16),...]
    psum x1 -> x0, blocking collectives: 129 us -> none  [body(): shrunk = lax.psum(shrink_part, ('tensor', 'seq')).astype(jnp.bfloat16)]
    all_to_all x2 -> x0, waiting for transfers between devices: 78.8 us -> none  [the longest x1 43.5 us: body(): lax.all_to_all(down_send.reshape(owner_count, CAP, rank_extent, partial_r...]
    dot_general x7 -> x0, matrix products: 46.5 us -> none  [the longest x1 13.4 us: attend(): jnp.einsum('tlhd,kld->tlhk', queries, key_rows, preferred_element_type=jn...]
    all_gather x3 -> x0, blocking collectives: 45.5 us -> none  [the longest x1 16.1 us: body(): lax.all_gather(adapter_per_request, 'dp', axis=0, tiled=True)]
    all_to_all x2 -> x0, starting transfers between devices: 14.8 us -> none  [the longest x1 8.09 us: body(): lax.all_to_all(down_send.reshape(owner_count, CAP, rank_extent, partial_r...]
    reduce_sum x6 -> x1, other arithmetic: 12.5 us -> 0.85 us  [body(): jnp.sum(jnp.where(adapter_per_request[0][:, None] == jnp.arange(128, dtyp...]
    unnamed x23 -> x2, local copies, waits for them, and re-layouts: 11 us -> 2.49 us
  transfers between devices with their start and end apart: 5 -> 0, of which waited for: 2 -> 0; matrix products, arithmetic and copies ran while one was open for 16% -> 0% of each run, Pallas kernels for 0% -> 0%
where the time goes in v1:
time: 148 us
  Pallas kernels  141 us (95%)
  other arithmetic  4.38 us (3%)
  local copies, waits for them, and re-layouts  2.49 us (2%)
    pallas_call x1, Pallas kernels, body(): pl.pallas_call(kernel, out_shape=jax.ShapeDtypeStruct((TOK, COLS), BF16),...  141 us

profile of v1, /device:TPU:1, one launch (start us, length us, event | category | flops | bytes accessed | tf_op | source)
XLA Modules:
  0.0 147.5 jit_solution(8161812014927392872)
XLA Ops:
  0.0 0.9 reduce-window_clone.1
  0.9 0.7 sub.4
  1.5 0.8 select_reduce_fusion
  2.4 0.7 pad_add_fusion.meta
  3.1 0.8 copy.15
  3.8 1.3 bitcast_select_fusion.pages
  5.2 140.6 %layer.1 = bf16[640,256]{1,0:T(8,128)(2,1)} custom-call(bf16[640,2048]{1,0:T(8,128)(2,1)} %hidden.1, bf16[2048,8,256]{2,1,0:T(8,128)(2,1)} %weight.1, bf16[4,64,2048]{2,1,0:T(8,128)(2,1)} %down.1, bf16[4,64,1024]{2,1,0:T(8,128)(2,1)} %bitcast.12, s32[8,128]{1,0:T(8,128)} %pad_add_fusion.meta, s32[32,16]{1,0:T(8,128)} %bitcast_select_fusion.pages, ...), custom_call_target="tpu_custom_call" | custom-call | tf_op jit(solution)/shard_map/layer/pallas_call | solution.py:611
  145.8 1.7 %copy.17 = bf16[640,1,256]{2,0,1:T(8,128)(2,1)} copy(bf16[640,1,256]{2,0,1:T(8,128)(2,1)} %bitcast.11) | data formatting | bytes 655360
  (2 shorter events, 0.0 us)

commit v2 on v1

v2 whole, which is shorter than its diff:
```python
import functools
import math

import jax
import jax.numpy as jnp
from jax import lax
from jax.experimental import pallas as pl
from jax.experimental.pallas import tpu as pltpu
from jax.sharding import PartitionSpec as P

MESH = pl.DeviceIdType.MESH
BF16, F32, I32 = jnp.bfloat16, jnp.float32, jnp.int32

TOK = 640
HALF = 320
WIDTH = 2048
QUARTER = 512
COLS = 256
HEAD = 128
RANK = 64
KEYS = 4096
NEW_EACH = 160
WINDOW = 384
CHUNK = 512
TILE = 320
NEGATIVE = -1e30
ORDER = (0, 1, -1, 2, -2, 3, -3, 4)
EXPONENT = HEAD**-0.5 * math.log2(math.e)


def iota(shape, dimension):
    return lax.broadcasted_iota(I32, shape, dimension)


def as_bf16(condition):
    return jnp.where(condition, 1.0, 0.0).astype(BF16)


def lanes(rows):
    return lax.broadcasted_iota(I32, (rows, 128), 1)


def token_slots(meta, first, rows):
    position = lax.broadcasted_iota(I32, (rows, 128), 0) + first
    inside = (position >= meta[0:1, :]) & (position < meta[1:2, :])
    slot = jnp.where(inside, meta[2:3, :].astype(F32), 0.0)
    return jnp.broadcast_to(jnp.sum(slot, axis=1, keepdims=True), (rows, 128)).astype(I32)


def kernel(
    hidden,
    weight,
    down,
    up,
    pool,
    adapters,
    lengths,
    tables,
    used,
    cache_k,
    cache_v,
    new_k,
    new_v,
    out,
    hid,
    chunks,
    wraw,
    wf32,
    wk,
    downs,
    ups,
    metas,
    part_send,
    part_core,
    part_sum,
    part_y,
    part_relay,
    query,
    shr,
    shr_core,
    shr_sum,
    shr_y,
    shr_x,
    shr_all,
    shr_z,
    shr_packed,
    shr_wide,
    slots_here,
    bias,
    keys,
    values,
    scores,
    load_sem,
    w_sem,
    meta_s,
    meta_r,
    hid_s,
    hid_r,
    up_s,
    up_r,
    x_s,
    x_r,
    core_s,
    core_r,
    y_s,
    y_r,
    red_s,
    red_r,
):
    z = lax.axis_index("dp")
    t = lax.axis_index("tensor")
    x = lax.axis_index("seq")
    y, core = t // 2, t % 2

    def at_z(d):
        return {"dp": lax.rem(z + d + 8, 8)}

    def at_x(d):
        return {"seq": lax.rem(x + d, 4)}

    def at_y(d):
        return {"tensor": lax.rem(y + d, 4) * 2 + core}

    sibling = {"tensor": y * 2 + 1 - core}
    barrier = pltpu.get_barrier_semaphore()
    peers = [at_z(d) for d in range(1, 8)] + [at_x(d) for d in range(1, 4)]
    peers += [at_y(d) for d in range(1, 4)] + [sibling]
    for peer in peers:
        pl.semaphore_signal(barrier, inc=1, device_id=peer, device_id_type=MESH)
    pl.semaphore_wait(barrier, len(peers))

    def send(src, dst, s, r, peer):
        copy = pltpu.make_async_remote_copy(
            src_ref=src, dst_ref=dst, send_sem=s, recv_sem=r, device_id=peer, device_id_type=MESH
        )
        copy.start()
        return copy

    def local(src, dst, sem):
        copy = pltpu.make_async_copy(src, dst, sem)
        copy.start()
        return copy

    quarter = pl.ds(pl.multiple_of(x * QUARTER, QUARTER), QUARTER)

    ring = {}
    for u in range(2):
        rows = pl.ds(u * HALF, HALF)
        for way in range(2):
            ring[way, 1, u] = send(
                hidden.at[rows, quarter],
                chunks.at[z, rows],
                hid_s.at[way, 0, u],
                hid_r.at[way, 0, u],
                at_z(1 - 2 * way),
            )
    row, column = iota((32, 128), 0), iota((32, 128), 1)

    def spread_out(ref, matrix):
        wide = jnp.broadcast_to(ref[...], (8, ref.shape[1])).astype(F32).astype(BF16)
        return jnp.dot(wide, as_bf16(matrix), preferred_element_type=F32)

    finish = spread_out(lengths, (row <= column) & (column < 32))
    starts = spread_out(lengths, (row < column) & (column < 32))
    finish_high = spread_out(lengths, (row <= column - 64) & (column < 96))
    starts_high = spread_out(lengths, (row < column - 64) & (column < 96))
    adapter = spread_out(adapters, row == column)[0:1, :]
    named = iota((128, 128), 0).astype(F32) == adapter
    slots = spread_out(pool, named)
    which = iota((8, 128), 0)
    about = jnp.where(which == 0, starts, 0.0)
    for n, values_here in ((1, finish), (2, slots), (3, starts_high), (4, finish_high)):
        about = jnp.where(which == n, values_here, about)
    metas[z] = about.astype(I32)
    meta_copies = [
        send(metas.at[z], metas.at[z], meta_s.at[d], meta_r.at[d], at_z(d)) for d in range(1, 8)
    ]
    own = []
    own_hid = local(hidden, hid, load_sem.at[1])
    own_chunk = local(hidden.at[:, quarter], chunks.at[z], load_sem.at[2])
    w_copies = [
        local(weight.at[pl.ds(i * 256, 256)], wraw.at[pl.ds(i * 256, 256)], w_sem.at[i])
        for i in range(8)
    ]
    mine4 = pl.ds(x * 4, 4)
    down_copies = []
    for d in range(1, 4):
        to = lax.rem(x + d, 4)
        down_copies.append(
            send(
                down.at[:, :, pl.ds(pl.multiple_of(to * QUARTER, QUARTER), QUARTER)],
                downs.at[mine4],
                x_s.at[0, d],
                x_r.at[0, d],
                at_x(d),
            )
        )
    own_down = local(down.at[:, :, quarter], downs.at[mine4], load_sem.at[3])
    def serve_hidden(step, u):
        rows = pl.ds(u * HALF, HALF)
        for way in range(2):
            if step == 4 and u != way:
                continue
            ring[way, step, u].wait_recv()
            if step < 3 or (step == 3 and u == way):
                origin = lax.rem(z + (2 * way - 1) * step + 8, 8)
                ring[way, step + 1, u] = send(
                    chunks.at[origin, rows],
                    chunks.at[origin, rows],
                    hid_s.at[way, step, u],
                    hid_r.at[way, step, u],
                    at_z(1 - 2 * way),
                )

    up_ring = {}

    def up_part(origin, h, r):
        return ups.at[origin, h, pl.ds(r * 8, 8)]

    def start_up(h, r):
        for way in range(2):
            up_ring[way, 1, h, r] = send(
                up_part(z, h, r),
                up_part(z, h, r),
                up_s.at[way, 0, h, r],
                up_r.at[way, 0, h, r],
                at_z(1 - 2 * way),
            )

    def serve_up(step, h, r):
        for way in range(2):
            if step == 4 and r != way:
                continue
            up_ring[way, step, h, r].wait_recv()
            if step < 3 or (step == 3 and r == way):
                origin = lax.rem(z + (2 * way - 1) * step + 8, 8)
                up_ring[way, step + 1, h, r] = send(
                    up_part(origin, h, r),
                    up_part(origin, h, r),
                    up_s.at[way, step, h, r],
                    up_r.at[way, step, h, r],
                    at_z(1 - 2 * way),
                )

    for i in range(8):
        w_copies[i].wait()

    @pl.loop(0, 16)
    def _(i):
        first = pl.multiple_of(i * 128, 128)
        wide = wraw[pl.ds(first, 128)].astype(F32).reshape(1024, COLS)
        wf32[pl.ds(0, 1024)] = wide[:, :HEAD]
        wf32[pl.ds(1024, 1024)] = wide[:, HEAD:]
        for k in range(8):
            for g in range(2):
                wk[k, pl.ds(first, 128), pl.ds(g * HEAD, HEAD)] = wf32[
                    pl.ds(g * 1024 + k, 128, stride=8), :
                ].astype(BF16)

    own_hid.wait()

    def product(head, rows):
        return jnp.dot(hid[rows], wk[head], preferred_element_type=F32)

    part_copies = []
    for d in (1, 0, 2, 3):
        target = lax.rem(y + 1 + d, 4)

        @pl.loop(0, 2)
        def _(i):
            rows = pl.ds(pl.multiple_of(i * HALF, HALF), HALF)
            part_send[d, rows] = product(target * 2 + 1 - core, rows)

        part_copies.append(
            send(part_send.at[d], part_core.at[d], core_s.at[d], core_r.at[d], sibling)
        )
    serve_hidden(1, 0)
    y_copies = []
    relay_copies = []
    for d in (1, 0, 2, 3):
        target = lax.rem(y + 1 + d, 4)
        part_copies[(1, 0, 2, 3).index(d)].wait_recv()

        @pl.loop(0, 2)
        def _(i):
            rows = pl.ds(pl.multiple_of(i * HALF, HALF), HALF)
            part_sum[d, rows] = product(target * 2 + core, rows) + part_core[d, rows]

        if d == 1:
            for way in range(2):
                rows = pl.ds(way * HALF, HALF)
                relay_copies.append(
                    send(
                        part_sum.at[1, rows],
                        part_relay.at[way],
                        y_s.at[way],
                        y_r.at[way],
                        at_y(1 + 2 * way),
                    )
                )
    for way in range(2):
        rows = pl.ds(way * HALF, HALF)
        relay_copies[way].wait_recv()
        part_sum[2 * way, rows] += part_relay[way]
        y_copies.append(
            send(
                part_sum.at[2 * way],
                part_y.at[way],
                y_s.at[2 + way],
                y_r.at[2 + way],
                at_y(1 + 2 * way),
            )
        )
    serve_hidden(1, 1)

    for copy in meta_copies:
        copy.wait_recv()
    own_down.wait()
    own_chunk.wait()
    for copy in down_copies:
        copy.wait_recv()
    up_copies = []
    for h in range(2):
        for d in range(1, 4):
            to = lax.rem(x + d, 4)
            up_copies.append(
                send(
                    up.at[:, :, pl.ds(pl.multiple_of(to * COLS + h * HEAD, HEAD), HEAD)],
                    ups.at[z, h, mine4],
                    x_s.at[1 + h, d],
                    x_r.at[1 + h, d],
                    at_x(d),
                )
            )
        own.append(
            local(
                up.at[:, :, pl.ds(pl.multiple_of(x * COLS + h * HEAD, HEAD), HEAD)],
                ups.at[z, h, mine4],
                load_sem.at[4 + h],
            )
        )

    def shrink(place):
        origin = lax.rem(z + ORDER[place] + 8, 8)
        about = metas[origin]

        def block(first):
            rows = pl.ds(first, 160)
            product = lax.dot_general(
                chunks[origin, rows],
                downs[...].reshape(1024, QUARTER),
                (((1,), (1,)), ((), ())),
                preferred_element_type=F32,
            )
            slot = token_slots(about, first, 160) - z * 16
            half = lanes(160) // RANK
            total = jnp.zeros((160, 128), F32)
            for j in range(8):
                piece = product[:, j * 128 : (j + 1) * 128]
                total = total + jnp.where(slot == 2 * j + half, piece, 0.0)
            return total + pltpu.roll(total, RANK, 1)

        @pl.loop(0, 2)
        def _(i):
            first = pl.multiple_of(i * 160, 160)
            low, high = block(first), block(first + HALF)
            shr[place, pl.ds(first, 160)] = jnp.where(lanes(160) < RANK, low, high)

    other_rows = pl.ds(pl.multiple_of((1 - core) * 160, 32), 160)
    core_rows = pl.ds(pl.multiple_of(core * 160, 32), 160)
    batches = (pl.ds(0, 5), pl.ds(5, 3))
    red = []

    def finish_all(copies):
        for copy in copies:
            copy.wait_recv()
        red.extend(copies)

    def reduce_core(b):
        return [
            send(
                shr.at[batches[b], other_rows],
                shr_core.at[batches[b]],
                red_s.at[0, b, 0],
                red_r.at[0, b, 0],
                sibling,
            )
        ]

    def reduce_y(b, before):
        finish_all(before)
        batch = batches[b]
        shr_sum[batch] = shr[batch, core_rows] + shr_core[batch]
        copies = []
        for d in range(1, 4):
            rows = pl.ds(pl.multiple_of(lax.rem(y + d, 4) * 40, 8), 40)
            copies.append(
                send(
                    shr_sum.at[batch, rows],
                    shr_y.at[d - 1, batch],
                    red_s.at[1, b, d],
                    red_r.at[1, b, d],
                    at_y(d),
                )
            )
        return copies

    def reduce_x(b, before):
        finish_all(before)
        batch = batches[b]
        mine = shr_sum[batch, pl.ds(pl.multiple_of(y * 40, 8), 40)]
        shr_x[x, batch] = mine + shr_y[0, batch] + shr_y[1, batch] + shr_y[2, batch]
        return [
            send(
                shr_x.at[x, batch],
                shr_x.at[x, batch],
                red_s.at[2, b, d],
                red_r.at[2, b, d],
                at_x(d),
            )
            for d in range(1, 4)
        ]

    def reduce_z(b, before):
        finish_all(before)
        batch = batches[b]
        total = shr_x[0, batch] + shr_x[1, batch] + shr_x[2, batch] + shr_x[3, batch]
        shr_all[batch] = total.astype(BF16).astype(F32)
        return [
            send(
                shr_all.at[place],
                shr_z.at[place],
                red_s.at[3, b, place],
                red_r.at[3, b, place],
                at_z(ORDER[place]),
            )
            for place in ((1, 2, 3, 4) if b == 0 else (5, 6, 7))
        ]

    shrink(0)
    shrink(1)
    serve_hidden(2, 0)
    serve_hidden(2, 1)
    shrink(2)
    own[0].wait()
    own[1].wait()
    for copy in up_copies:
        copy.wait_recv()

    first_lanes = pl.ds(0, HEAD)

    def old_rows(d):
        return pl.ds(pl.multiple_of(lax.rem(x + d, 4) * 1024, 1024), 1024)

    def new_rows(d):
        return pl.ds(pl.multiple_of(KEYS + lax.rem(x + d, 4) * NEW_EACH, 32), NEW_EACH)

    def place_of(n, d):
        rows = old_rows(d) if n < 2 else new_rows(d)
        return keys.at[rows, first_lanes] if n % 2 == 0 else values.at[rows]

    kv_copies = {}
    for n, src in enumerate((cache_k, cache_v, new_k, new_v)):
        for way in range(2):
            kv_copies[n, way] = send(
                src, place_of(n, 0), x_s.at[3 + n, way], x_r.at[3 + n, way], at_x(1 + 2 * way)
            )
        own.append(local(src, place_of(n, 0), load_sem.at[6 + n]))

    def pass_on():
        for n in range(4):
            way = n % 2
            kv_copies[n, way].wait_recv()
            arrived = place_of(n, 3 - 2 * way)
            kv_copies[n, 2] = send(
                arrived, arrived, x_s.at[3 + n, 2], x_r.at[3 + n, 2], at_x(1 + 2 * way)
            )

    shrink(3)
    shrink(4)
    first_core = reduce_core(0)

    about = metas[z]
    row, column = iota((128, 32), 0), iota((128, 32), 1)
    listed = row - 64 == column
    for i in range(16):
        listed = listed | ((tables[i : i + 1, :] == row) & (used[...] > i) & (row < 64))
    listed = as_bf16(listed)

    @pl.loop(0, 4)
    def _(i):
        first = pl.multiple_of(i * 160, 160)
        rows = pl.ds(first, 160)
        position = lax.broadcasted_iota(I32, (160, 128), 0) + first
        member = (position >= about[0:1, :]) & (position < about[1:2, :])
        count = lax.dot_general(
            as_bf16(member)[:, :32], listed, (((1,), (1,)), ((), ())), preferred_element_type=F32
        )
        free = (count > 0.5) | (lanes(160) >= 96)
        bias[rows] = jnp.where(free, 0.0, NEGATIVE).astype(BF16)
        slots_here[rows] = token_slots(about, first, 160)
        shifted = (position >= about[3:4, :]) & (position < about[4:5, :])
        keys[pl.ds(pl.multiple_of(KEYS + i * 160, 32), 160), pl.ds(HEAD, 128)] = jnp.where(
            shifted, 1.0, 0.0
        ).astype(BF16)

    @pl.loop(0, 16)
    def _(i):
        first = pl.multiple_of(i * 256, 256)
        page = (lax.broadcasted_iota(I32, (256, 128), 0) + first) // 64
        keys[pl.ds(first, 256), pl.ds(HEAD, 128)] = jnp.where(
            page == lanes(256), 1.0, 0.0
        ).astype(BF16)

    first_y = reduce_y(0, first_core)
    serve_hidden(3, 0)
    serve_hidden(3, 1)
    start_up(0, 0)
    start_up(0, 1)
    first_x = reduce_x(0, first_y)
    shrink(5)
    shrink(6)
    pass_on()
    start_up(1, 0)
    start_up(1, 1)
    first_z = reduce_z(0, first_x)
    serve_hidden(4, 0)
    serve_hidden(4, 1)
    shrink(7)
    last_core = reduce_core(1)
    serve_up(1, 0, 0)
    serve_up(1, 0, 1)
    last_y = reduce_y(1, last_core)
    serve_up(1, 1, 0)
    serve_up(1, 1, 1)
    last_x = reduce_x(1, last_y)
    serve_up(2, 0, 0)
    serve_up(2, 0, 1)
    last_z = reduce_z(1, last_x)
    finish_all(first_z)
    finish_all(last_z)
    total = shr_all[0]
    for place in range(1, 8):
        total = total + shr_z[place]
    final_rows = pl.ds(pl.multiple_of(core * 160 + y * 40, 8), 40)
    shr_packed[final_rows] = total
    red_f = [
        send(
            shr_packed.at[final_rows],
            shr_packed.at[final_rows],
            red_s.at[4, 0, d],
            red_r.at[4, 0, d],
            at_y(d),
        )
        for d in range(1, 4)
    ]
    serve_up(2, 1, 0)
    serve_up(2, 1, 1)
    finish_all(red_f)
    core_final = send(
        shr_packed.at[core_rows],
        shr_packed.at[core_rows],
        red_s.at[4, 1, 0],
        red_r.at[4, 1, 0],
        sibling,
    )
    serve_up(3, 0, 0)
    serve_up(3, 0, 1)
    for copy in y_copies:
        copy.wait_recv()

    @pl.loop(0, 2)
    def _(i):
        rows = pl.ds(pl.multiple_of(i * HALF, HALF), HALF)
        total = part_sum[3, rows] + part_y[0, rows] + part_y[1, rows]
        query[0, rows] = total[:, :HEAD]
        query[1, rows] = total[:, HEAD:]

    finish_all([core_final])
    packed = shr_packed[...]
    turned = pltpu.roll(packed, RANK, 1)
    shr_wide[pl.ds(0, HALF)] = jnp.where(lanes(HALF) < RANK, packed, turned)
    shr_wide[pl.ds(HALF, HALF)] = jnp.where(lanes(HALF) < RANK, turned, packed)

    def expand(origin, h):
        origin = lax.rem(origin + 8, 8)

        @pl.loop(0, 4)
        def _(i):
            rows = pl.ds(pl.multiple_of(i * 160, 160), 160)
            slot = slots_here[rows] - origin * 16
            wide = shr_wide[rows]
            half = lanes(160) // RANK
            spread = jnp.concatenate(
                [jnp.where(slot == 2 * j + half, wide, 0.0).astype(BF16) for j in range(8)], axis=1
            )
            query[h, rows] += jnp.dot(
                spread, ups[origin, h].reshape(1024, HEAD), preferred_element_type=F32
            )

    def attend(h, i):
        first = i * TILE
        begin_new = max(first - 64, 0)
        rows = pl.ds(first, TILE)
        left = jnp.concatenate([query[h, rows].astype(BF16), bias[rows]], axis=1)
        highest = jnp.full((TILE, 128), NEGATIVE, F32)
        for c in range(KEYS // CHUNK):
            piece = lax.dot_general(
                left,
                keys[pl.ds(c * CHUNK, CHUNK)],
                (((1,), (1,)), ((), ())),
                preferred_element_type=F32,
            )
            scores[:, pl.ds(c * CHUNK, CHUNK)] = piece
            for j in range(CHUNK // 128):
                highest = jnp.maximum(highest, piece[:, j * 128 : (j + 1) * 128])
        piece = lax.dot_general(
            left,
            keys[pl.ds(KEYS + begin_new, WINDOW)],
            (((1,), (1,)), ((), ())),
            preferred_element_type=F32,
        )
        position = lax.broadcasted_iota(I32, (TILE, WINDOW), 0) + first
        piece = jnp.where(
            lax.broadcasted_iota(I32, (TILE, WINDOW), 1) + begin_new <= position, piece, NEGATIVE
        )
        scores[:, pl.ds(KEYS, WINDOW)] = piece
        for j in range(WINDOW // 128):
            highest = jnp.maximum(highest, piece[:, j * 128 : (j + 1) * 128])
        top = jnp.broadcast_to(jnp.max(highest, axis=1, keepdims=True), (TILE, 128))
        sums = jnp.zeros((TILE, 128), F32)
        total = jnp.zeros((TILE, HEAD), F32)
        bounds = [(c * CHUNK, c * CHUNK, CHUNK) for c in range(KEYS // CHUNK)]
        bounds.append((KEYS, KEYS + begin_new, WINDOW))
        for begin, place, size in bounds:
            parts = []
            for j in range(size // 128):
                e = jnp.exp2((scores[:, pl.ds(begin + j * 128, 128)] - top) * EXPONENT)
                sums = sums + e
                parts.append(e.astype(BF16))
            total = total + jnp.dot(
                jnp.concatenate(parts, axis=1),
                values[pl.ds(place, size)],
                preferred_element_type=F32,
            )
        out[rows, pl.ds(h * HEAD, HEAD)] = (
            total / jnp.sum(sums, axis=1, keepdims=True)
        ).astype(BF16)

    for d in (0, -1, 1, -2, 2, -3, 3):
        expand(z + d, 0)
    serve_up(4, 0, 0)
    serve_up(4, 0, 1)
    expand(z + 4, 0)
    for n in range(4):
        kv_copies[n, 1 - n % 2].wait_recv()
        kv_copies[n, 2].wait_recv()
    for copy in own[2:]:
        copy.wait()
    attend(0, 0)
    serve_up(3, 1, 0)
    serve_up(3, 1, 1)
    attend(0, 1)
    for d in (0, -1, 1, -2, 2, -3, 3):
        expand(z + d, 1)
    serve_up(4, 1, 0)
    serve_up(4, 1, 1)
    expand(z + 4, 1)
    attend(1, 0)
    attend(1, 1)

    for copies in (
        list(ring.values()),
        list(up_ring.values()),
        meta_copies,
        down_copies,
        up_copies,
        part_copies,
        y_copies,
        relay_copies,
        list(kv_copies.values()),
        red,
    ):
        for copy in copies:
            copy.wait_send()


def body(
    hidden,
    query_weight,
    adapter_down_factor,
    adapter_up_factor,
    adapter_pool_slot,
    adapter_per_request,
    incoming_length,
    prefix_page_table,
    page_used_count,
    paged_key_cache,
    paged_value_cache,
    incoming_keys,
    incoming_values,
):
    vmem = pl.BlockSpec(memory_space=pltpu.VMEM)
    anywhere = pl.BlockSpec(memory_space=pl.ANY)
    dma = pltpu.SemaphoreType.DMA
    result = pl.pallas_call(
        kernel,
        out_shape=jax.ShapeDtypeStruct((TOK, COLS), BF16),
        in_specs=[anywhere] * 4 + [vmem] * 5 + [anywhere] * 4,
        out_specs=vmem,
        scratch_shapes=[
            pltpu.VMEM((TOK, WIDTH), BF16),
            pltpu.VMEM((8, TOK, QUARTER), BF16),
            pltpu.VMEM((WIDTH, 8, COLS), BF16),
            pltpu.VMEM((2048, HEAD), F32),
            pltpu.VMEM((8, WIDTH, COLS), BF16),
            pltpu.VMEM((16, RANK, QUARTER), BF16),
            pltpu.VMEM((8, 2, 16, RANK, HEAD), BF16),
            pltpu.VMEM((8, 8, 128), I32),
            pltpu.VMEM((4, TOK, COLS), F32),
            pltpu.VMEM((4, TOK, COLS), F32),
            pltpu.VMEM((4, TOK, COLS), F32),
            pltpu.VMEM((2, TOK, COLS), F32),
            pltpu.VMEM((2, HALF, COLS), F32),
            pltpu.VMEM((2, TOK, HEAD), F32),
            pltpu.VMEM((8, HALF, 128), F32),
            pltpu.VMEM((8, 160, 128), F32),
            pltpu.VMEM((8, 160, 128), F32),
            pltpu.VMEM((3, 8, 40, 128), F32),
            pltpu.VMEM((4, 8, 40, 128), F32),
            pltpu.VMEM((8, 40, 128), F32),
            pltpu.VMEM((8, 40, 128), F32),
            pltpu.VMEM((HALF, 128), F32),
            pltpu.VMEM((TOK, 128), F32),
            pltpu.VMEM((TOK, 128), I32),
            pltpu.VMEM((TOK, 128), BF16),
            pltpu.VMEM((KEYS + TOK, 2 * HEAD), BF16),
            pltpu.VMEM((KEYS + TOK, HEAD), BF16),
            pltpu.VMEM((TILE, KEYS + WINDOW), F32),
            dma((10,)),
            dma((8,)),
            dma((8,)),
            dma((8,)),
            dma((2, 4, 2)),
            dma((2, 4, 2)),
            dma((2, 4, 2, 2)),
            dma((2, 4, 2, 2)),
            dma((7, 4)),
            dma((7, 4)),
            dma((4,)),
            dma((4,)),
            dma((4,)),
            dma((4,)),
            dma((5, 2, 8)),
            dma((5, 2, 8)),
        ],
        compiler_params=pltpu.CompilerParams(
            collective_id=0, has_side_effects=True, vmem_limit_bytes=63 << 20
        ),
        name="layer",
    )(
        hidden,
        query_weight,
        adapter_down_factor,
        adapter_up_factor.reshape(4, RANK, 1024),
        adapter_pool_slot.reshape(1, 128),
        adapter_per_request,
        incoming_length,
        prefix_page_table[0].T,
        page_used_count,
        paged_key_cache.reshape(1024, HEAD),
        paged_value_cache.reshape(1024, HEAD),
        incoming_keys.reshape(NEW_EACH, HEAD),
        incoming_values.reshape(NEW_EACH, HEAD),
    )
    return result.reshape(TOK, 1, COLS)


def solution(mesh):
    return jax.shard_map(
        body,
        mesh=mesh,
        in_specs=(
            P("dp", "tensor"),
            P("tensor", None, "seq"),
            P(("dp", "seq"), None, "tensor"),
            P(("dp", "seq"), None, "tensor", None),
            P(),
            P("dp", None),
            P("dp", None),
            P("dp", None, None),
            P("dp", None),
            P("dp", "seq", None, "tensor", None),
            P("dp", "seq", None, "tensor", None),
            P(("dp", "seq"), "tensor", None),
            P(("dp", "seq"), "tensor", None),
        ),
        out_specs=P("dp", "tensor", "seq"),
        check_vma=False,
    )
```

time: 148 us -> 136 us (0.919)
  Pallas kernels: 141 us -> 134 us
  other arithmetic: 4.38 us -> 0 us
    pallas_call x1, Pallas kernels: 141 us -> 134 us  [body(): pl.pallas_call(kernel, out_shape=jax.ShapeDtypeStruct((TOK, COLS), BF16),...]
where the time goes in v2:
time: 136 us
  Pallas kernels  134 us (99%)
  local copies, waits for them, and re-layouts  1.72 us (1%)
    pallas_call x1, Pallas kernels, body(): pl.pallas_call(kernel, out_shape=jax.ShapeDtypeStruct((TOK, COLS), BF16),...  134 us

profile of v2, /device:TPU:1, one launch (start us, length us, event | category | flops | bytes accessed | tf_op | source)
XLA Modules:
  0.0 136.1 jit_solution(12483980416573566457)
XLA Ops:
  0.0 134.4 %layer.1 = bf16[640,256]{1,0:T(8,128)(2,1)} custom-call(bf16[640,2048]{1,0:T(8,128)(2,1)} %hidden.1, bf16[2048,8,256]{2,1,0:T(8,128)(2,1)} %weight.1, bf16[4,64,2048]{2,1,0:T(8,128)(2,1)} %down.1, bf16[4,64,1024]{2,1,0:T(8,128)(2,1)} %bitcast.11, s32[1,128]{1,0:T(1,128)} %bitcast.17, s32[1,32]{1,0:T(1,128)} %adapters.1, s32[1,32]{1,0:T(1,128)} %lengths.1, ...), custom_call_target="tpu_custom_call" | custom-call | tf_op jit(solution)/shard_map/layer/pallas_call | solution.py:706
  134.4 1.7 %copy.15 = bf16[640,1,256]{2,0,1:T(8,128)(2,1)} copy(bf16[640,1,256]{2,0,1:T(8,128)(2,1)} %bitcast.10) | data formatting | bytes 655360

commit v3 on v2

--- a/solution.py
+++ b/solution.py
@@ -521,6 +521,16 @@
     shrink(5)
     shrink(6)
     pass_on()
+    for copy in y_copies:
+        copy.wait_recv()
+
+    @pl.loop(0, 2)
+    def _(i):
+        rows = pl.ds(pl.multiple_of(i * HALF, HALF), HALF)
+        total = part_sum[3, rows] + part_y[0, rows] + part_y[1, rows]
+        query[0, rows] = total[:, :HEAD]
+        query[1, rows] = total[:, HEAD:]
+
     start_up(1, 0)
     start_up(1, 1)
     first_z = reduce_z(0, first_x)
@@ -534,8 +544,6 @@
     serve_up(1, 1, 0)
     serve_up(1, 1, 1)
     last_x = reduce_x(1, last_y)
-    serve_up(2, 0, 0)
-    serve_up(2, 0, 1)
     last_z = reduce_z(1, last_x)
     finish_all(first_z)
     finish_all(last_z)
@@ -554,8 +562,6 @@
         )
         for d in range(1, 4)
     ]
-    serve_up(2, 1, 0)
-    serve_up(2, 1, 1)
     finish_all(red_f)
     core_final = send(
         shr_packed.at[core_rows],
@@ -564,19 +570,9 @@
         red_r.at[4, 1, 0],
         sibling,
     )
-    serve_up(3, 0, 0)
-    serve_up(3, 0, 1)
-    for copy in y_copies:
-        copy.wait_recv()
-
-    @pl.loop(0, 2)
-    def _(i):
-        rows = pl.ds(pl.multiple_of(i * HALF, HALF), HALF)
-        total = part_sum[3, rows] + part_y[0, rows] + part_y[1, rows]
-        query[0, rows] = total[:, :HEAD]
-        query[1, rows] = total[:, HEAD:]
-
+    serve_up(2, 0, 0)
     finish_all([core_final])
+    serve_up(2, 0, 1)
     packed = shr_packed[...]
     turned = pltpu.roll(packed, RANK, 1)
     shr_wide[pl.ds(0, HALF)] = jnp.where(lanes(HALF) < RANK, packed, turned)
@@ -647,22 +643,29 @@
             total / jnp.sum(sums, axis=1, keepdims=True)
         ).astype(BF16)
 
-    for d in (0, -1, 1, -2, 2, -3, 3):
-        expand(z + d, 0)
-    serve_up(4, 0, 0)
-    serve_up(4, 0, 1)
-    expand(z + 4, 0)
+    serve_up(2, 1, 0)
+    serve_up(2, 1, 1)
     for n in range(4):
         kv_copies[n, 1 - n % 2].wait_recv()
         kv_copies[n, 2].wait_recv()
     for copy in own[2:]:
         copy.wait()
-    attend(0, 0)
+    for d in (0, -1, 1, -2, 2):
+        expand(z + d, 0)
+    serve_up(3, 0, 0)
+    serve_up(3, 0, 1)
+    for d in (0, -1, 1, -2, 2):
+        expand(z + d, 1)
     serve_up(3, 1, 0)
     serve_up(3, 1, 1)
+    for d in (-3, 3):
+        expand(z + d, 0)
+        expand(z + d, 1)
+    serve_up(4, 0, 0)
+    serve_up(4, 0, 1)
+    expand(z + 4, 0)
+    attend(0, 0)
     attend(0, 1)
-    for d in (0, -1, 1, -2, 2, -3, 3):
-        expand(z + d, 1)
     serve_up(4, 1, 0)
     serve_up(4, 1, 1)
     expand(z + 4, 1)

time: 136 us -> 131 us (0.963)
  Pallas kernels: 134 us -> 128 us
    pallas_call x1, Pallas kernels: 134 us -> 128 us  [body(): pl.pallas_call(kernel, out_shape=jax.ShapeDtypeStruct((TOK, COLS), BF16),...]
where the time goes in v3:
time: 131 us; the launch traced here: 130 us
  Pallas kernels  128 us (98%)
  local copies, waits for them, and re-layouts  1.72 us (1%)
    pallas_call x1, Pallas kernels, body(): pl.pallas_call(kernel, out_shape=jax.ShapeDtypeStruct((TOK, COLS), BF16),...  128 us

profile of v3, /device:TPU:1, one launch (start us, length us, event | category | flops | bytes accessed | tf_op | source)
XLA Modules:
  0.0 130.0 jit_solution(18399738582103057970)
XLA Ops:
  0.0 128.3 %layer.1 = bf16[640,256]{1,0:T(8,128)(2,1)} custom-call(bf16[640,2048]{1,0:T(8,128)(2,1)} %hidden.1, bf16[2048,8,256]{2,1,0:T(8,128)(2,1)} %weight.1, bf16[4,64,2048]{2,1,0:T(8,128)(2,1)} %down.1, bf16[4,64,1024]{2,1,0:T(8,128)(2,1)} %bitcast.11, s32[1,128]{1,0:T(1,128)} %bitcast.17, s32[1,32]{1,0:T(1,128)} %adapters.1, s32[1,32]{1,0:T(1,128)} %lengths.1, ...), custom_call_target="tpu_custom_call" | custom-call | tf_op jit(solution)/shard_map/layer/pallas_call | solution.py:709
  128.3 1.7 %copy.15 = bf16[640,1,256]{2,0,1:T(8,128)(2,1)} copy(bf16[640,1,256]{2,0,1:T(8,128)(2,1)} %bitcast.10) | data formatting | bytes 655360
